TPU v7x, 32 devices: a whole 2x2x4 slice. The times are simulated.
32 devices in a mesh: grp: 2 (over y), chan: 2 (over x), tm: 4 (over z), pol: 2 (over core).
Axes of the slice: x: 2, y: 2, z: 4, core: 2. Of those that a mesh axis runs over, the one named last changes fastest.
Arguments:
- voltages: bfloat16 [4, 2, 256, 32768], P('grp', 'pol', 'chan', 'tm'), parts along dimension 0, may hold values from -6 to 6
- taps_filter: float32 [16, 2048], replicated, may hold values from -1.5 to 1.5
- tile_a: int32 [14, 64], replicated, may hold values from 0 to 255
- tile_b: int32 [14, 64], replicated, may hold values from 0 to 255
- tile_owner: int32 [14], replicated, may hold values from 0 to 1, as said below
- tile_flags: int32 [14, 16], replicated, may hold values 0 or 1
Outputs:
- visibility: float32 [16, 256, 4, 2, 64, 128], P('pol', ('chan', 'tm'), 'grp'), parts along dimension 2
There are 2 independent parts, one for each index of `grp`. A program takes and returns all parts, laid end to end along the dimension named above; an argument that names none is the same for every part. Nothing has to cross between parts.
Inputs may be any that keep to these rules, and one draw needn't show every extreme that they name: `tile_owner`: one owner holds exactly 8 tiles and the other owner holds all the rest.
All inputs are finite; a program needn't handle non-finite values.
Results may differ from a plain program's by a relative error of at most 0.0035.
Values may be sent and summed in bfloat16 or wider, within the bound.
A program may use at most 128 MiB of HBM per device.

v0:
```python
import math

import jax
import jax.numpy as jnp
from jax import lax
from jax.experimental import pallas as pl
from jax.experimental.pallas import tpu as pltpu
from jax.sharding import PartitionSpec as P

AVG = 8
CAP = 8

radix_first = 16


def fourier(filtered):
    length = filtered.shape[-1]
    second = length // radix_first
    mode = lax.Precision.HIGH
    grid = filtered.reshape(filtered.shape[:-1] + (radix_first, second))
    outer = jnp.arange(radix_first, dtype=jnp.int32)
    inner = jnp.arange(second, dtype=jnp.int32)
    phase_one = (
        2.0
        * math.pi
        / radix_first
        * (outer[:, None] * outer[None, :] % radix_first).astype(jnp.float32)
    )
    phase_twist = 2.0 * math.pi / length * (outer[:, None] * inner[None, :]).astype(jnp.float32)
    phase_two = (
        2.0 * math.pi / second * (inner[:, None] * inner[None, :] % second).astype(jnp.float32)
    )
    scale = 1.0 / math.sqrt(length)
    cos_one, sin_one = (jnp.cos(phase_one), jnp.sin(phase_one))
    cos_twist, sin_twist = (jnp.cos(phase_twist), jnp.sin(phase_twist))
    cos_two, sin_two = (jnp.cos(phase_two) * scale, jnp.sin(phase_two) * scale)
    one = jnp.stack([jnp.stack([cos_one, sin_one]), jnp.stack([-sin_one, cos_one])])
    two = jnp.stack([jnp.stack([cos_two, sin_two]), jnp.stack([-sin_two, cos_two])])
    section = jnp.einsum("qrfk,rnkj->qnfj", one, grid, precision=mode)
    turned = jnp.stack(
        [
            section[0] * cos_twist + section[1] * sin_twist,
            section[1] * cos_twist - section[0] * sin_twist,
        ]
    )
    return jnp.einsum("qrgj,rnfj->qngf", two, turned, precision=mode)


def correlate_kernel(bands, stations, rows_ref, weight_ref, full_ref, out_ref):
    width = rows_ref.shape[1] // 2
    depth = full_ref.shape[-1]
    columns = lax.broadcasted_iota(jnp.int32, (2 * width, stations), 1)
    pick = jnp.where(rows_ref[0] == columns, 1.0, 0.0).astype(jnp.bfloat16)
    weight = weight_ref[0]
    for band in range(bands):
        source = jnp.concatenate(
            [
                full_ref[p, :, band, r].reshape(stations, depth)
                for p in range(2)
                for r in range(2)
            ],
            axis=-1,
        )
        picked = jnp.dot(pick, source, preferred_element_type=jnp.float32)
        parts = [picked[:, i * depth : (i + 1) * depth] for i in range(4)]
        left = [part[:width] * weight for part in parts]
        right = [part[width:] for part in parts]
        left_rows = jnp.concatenate(
            [
                jnp.concatenate([left[0], left[1]], axis=-1),
                jnp.concatenate([left[2], left[3]], axis=-1),
                jnp.concatenate([left[1], -left[0]], axis=-1),
                jnp.concatenate([left[3], -left[2]], axis=-1),
            ],
            axis=0,
        ).astype(jnp.bfloat16)
        right_rows = jnp.concatenate(
            [
                jnp.concatenate([right[0], right[1]], axis=-1),
                jnp.concatenate([right[2], right[3]], axis=-1),
            ],
            axis=0,
        ).astype(jnp.bfloat16)
        result = lax.dot_general(
            left_rows,
            right_rows,
            (((1,), (1,)), ((), ())),
            preferred_element_type=jnp.float32,
        ) * (1.0 / depth)
        out_ref[0, band] = result.reshape(2, 2, width, 2 * width)


def correlate(full, rows, weight):
    pols, sources, bands, parts, part_stations, depth = full.shape
    width = rows.shape[1] // 2
    step = 4 if bands % 4 == 0 else 1
    return pl.pallas_call(
        lambda *refs: correlate_kernel(step, sources * part_stations, *refs),
        grid=(bands // step, CAP),
        in_specs=[
            pl.BlockSpec((1, 2 * width, 1), lambda g, n: (n, 0, 0)),
            pl.BlockSpec((1, 1, depth), lambda g, n: (n, 0, 0)),
            pl.BlockSpec(
                (pols, sources, step, parts, part_stations, depth), lambda g, n: (0, 0, g, 0, 0, 0)
            ),
        ],
        out_specs=pl.BlockSpec(
            (1, step, 2, 2, width, 2 * width), lambda g, n: (n, g, 0, 0, 0, 0)
        ),
        out_shape=jax.ShapeDtypeStruct((CAP, bands, 2, 2, width, 2 * width), jnp.float32),
        compiler_params=pltpu.CompilerParams(vmem_limit_bytes=48 * 2**20),
    )(rows, weight, full)


def on_device(voltages, taps_filter, tile_a, tile_b, tile_owner, tile_flags):
    taps, length = taps_filter.shape
    stations = voltages.shape[2]
    frames = voltages.shape[3] // length
    chan_count = lax.axis_size("chan")
    time_count = lax.axis_size("tm")
    spectra_count = time_count * frames
    share = stations // time_count

    blocks = voltages.reshape(2, time_count, share, frames * length)
    blocks = lax.all_to_all(blocks, "tm", split_axis=1, concat_axis=1, tiled=True)
    blocks = blocks.reshape(2, time_count, share, frames, length)
    blocks = blocks.transpose(0, 2, 1, 3, 4).reshape(2, share, spectra_count, length)
    extended = jnp.pad(blocks, ((0, 0), (0, 0), (taps - 1, 0), (0, 0)))
    filtered = jnp.zeros((2, share, spectra_count, length), jnp.float32)
    for tap_index in range(taps):
        start = taps - 1 - tap_index
        filtered = filtered + taps_filter[tap_index] * extended[
            :, :, start : start + spectra_count
        ].astype(jnp.float32)
    spectra = fourier(filtered.reshape(2, share * spectra_count, length)).astype(jnp.bfloat16)

    owners = chan_count * time_count
    bands = length // (owners * AVG)
    outgoing = spectra.reshape(2, share, spectra_count, owners, bands, AVG)
    outgoing = outgoing.transpose(3, 4, 0, 1, 5, 2).reshape(
        owners, bands, 2, share, AVG * spectra_count
    )
    moved = lax.all_to_all(outgoing, ("chan", "tm"), split_axis=0, concat_axis=0, tiled=True)
    full = lax.all_gather(moved, "pol", axis=0)

    position = lax.axis_index("pol")
    held = tile_owner == position
    rank = jnp.cumsum(held.astype(jnp.int32)) - 1
    chosen = (
        (rank[None, :] == jnp.arange(CAP, dtype=jnp.int32)[:, None]) & held[None, :]
    ).astype(jnp.int32)
    pairs = jnp.concatenate([tile_a, tile_b], axis=1)
    rows = jnp.sum(chosen[:, :, None] * pairs[None], axis=1)[:, :, None]
    flags = jnp.sum(chosen[:, :, None] * tile_flags[None], axis=1)
    weight = jnp.tile(flags.astype(jnp.float32), (1, AVG))[:, None, :]
    return correlate(full, rows, weight)


def solution(mesh):
    return jax.shard_map(
        on_device,
        mesh=mesh,
        in_specs=(P("grp", "pol", "chan", "tm"), P(), P(), P(), P(), P()),
        out_specs=P("pol", ("chan", "tm"), "grp", None, None, None),
        check_vma=False,
    )
```

profile of v0, /device:TPU:0, one launch (start us, length us, event | category | flops | bytes accessed | tf_op | source)
XLA Modules:
  0.0 434.6 jit_solution(13082753197591950900)
XLA Ops:
  6.5 0.0 copy-start
  6.5 4.7 %copy.36 = bf16[2,4,32,8192]{3,2,0,1:T(8,128)(2,1)} copy(bf16[2,4,32,8192]{3,2,1,0:T(8,128)(2,1)} %bitcast.76) | data formatting | bytes 8388608 | tf_op jit(solution)/shard_map/reshape | solution.py:124
  11.2 6.3 %all-to-all-start = ((bf16[2,4,32,8192]{3,2,0,1:T(8,128)(2,1)}), bf16[2,4,32,8192]{3,2,0,1:T(8,128)(2,1)}, u32[]{:S(2)}, u32[]{:S(2)}) async-start(bf16[2,4,32,8192]{3,2,0,1:T(8,128)(2,1)} %copy.36), calls=%async_computation | async-start | bytes 8388608 | tf_op jit(solution)/shard_map/all_to_all | solution.py:125
  17.5 0.0 all-gather.3.cloned.1.call-start
  17.5 0.1 fusion.33
  17.6 0.1 fusion.31
  17.7 0.1 fusion.24
  17.7 0.3 fusion.20
  18.0 0.3 sine_multiply_fusion
  18.3 0.0 copy-done
  18.3 0.1 fusion.36
  18.4 92.5 %all-to-all-done = bf16[2,4,32,8192]{3,2,0,1:T(8,128)(2,1)} async-done(((bf16[2,4,32,8192]{3,2,0,1:T(8,128)(2,1)}), bf16[2,4,32,8192]{3,2,0,1:T(8,128)(2,1)}, u32[]{:S(2)}, u32[]{:S(2)}) %all-to-all-start) | async-done | bytes 4194336 | tf_op jit(solution)/shard_map/all_to_all | solution.py:125
  111.0 7.8 %reshape.302 = bf16[2,4,32,4,2048]{4,3,2,0,1:T(4,128)(2,1)} reshape(bf16[2,4,32,8192]{3,2,0,1:T(8,128)(2,1)} %all-to-all-done) | data formatting | bytes 8388608 | tf_op jit(solution)/shard_map/reshape | solution.py:126
  118.8 4.6 %copy.38 = bf16[2,32,4,4,2048]{4,1,3,2,0:T(8,128)(2,1)S(1)} copy(bf16[2,32,4,4,2048]{4,3,1,0,2:T(4,128)(2,1)} %bitcast.74) | data formatting | bytes 8388608 | tf_op jit(solution)/shard_map/transpose | solution.py:127
  123.4 12.8 %multiply_add_fusion = f32[2,32,16,2048]{3,1,2,0:T(8,128)S(1)} fusion(bf16[2,32,16,2048]{3,1,2,0:T(8,128)(2,1)S(1)} %bitcast.73, f32[2048]{0:T(1024)S(1)} %bitcast.91, f32[2048]{0:T(1024)S(1)} %bitcast.92, f32[2048]{0:T(1024)S(1)} %bitcast.78, f32[2048]{0:T(1024)S(1)} %bitcast.79, f32[2048]{0:T(1024)S(1)} %bitcast.80, f32[2048]{0:T(1024)S(1)} %bitcast.81, ...), kind=kLoop, calls=%fused_computation.21 | loop fusion | flops 98566144 | bytes 12713984 | tf_op jit(solution)/shard_map/add | solution.py:132
  136.1 8.5 %copy.52 = f32[2,32,16,2048]{3,0,2,1:T(2,128)} copy(f32[2,32,16,2048]{3,1,2,0:T(8,128)S(1)} %multiply_add_fusion) | data formatting | bytes 16777216 | tf_op jit(solution)/shard_map/reshape;reshape | solution.py:20
  144.7 11.5 %reshape.296 = f32[2,512,16,128,1]{3,2,0,1,4:T(8,128)} reshape(f32[2,32,16,2048]{3,0,2,1:T(2,128)} %copy.52) | data formatting | bytes 16777216 | tf_op jit(solution)/shard_map/reshape;reshape | solution.py:20
  156.2 6.1 %fusion.5 = f32[2,512,16,128]{3,2,0,1:T(8,128)S(1)} fusion(f32[2,512,16,128,1]{3,2,0,1,4:T(8,128)} %reshape.296, f32[1,2,16,16]{3,2,1,0:T(8,128)S(1)} %get-tuple-element.28, f32[1,2,16,16]{3,2,1,0:T(8,128)S(1)} %get-tuple-element.27), kind=kOutput, calls=%fused_computation.25 | convolution fusion | flops 402654208 | bytes 16781312 | tf_op jit(solution)/shard_map/qrfk,rnkj->qnfj/dot_general | solution.py:39
  162.3 0.9 multiply_add_fusion.1
  163.1 0.7 maximum_bitcast_fusion
  163.8 8.5 %fusion.4 = bf16[2,512,128,16]{2,1,0,3:T(8,128)(2,1)} fusion(f32[2,512,16,128,1]{3,2,0,1,4:T(8,128)S(1)} %maximum_bitcast_fusion, f32[1,2,128,128]{3,2,1,0:T(8,128)S(1)} %get-tuple-element.26, f32[1,2,128,128]{3,2,1,0:T(8,128)S(1)} %get-tuple-element.25), kind=kOutput, calls=%fused_computation.22 | convolution fusion | flops 3223388160 | bytes 12845056 | tf_op jit(solution)/shard_map/qrgj,rnfj->qngf/dot_general | solution.py:46
  172.3 7.9 %copy.42 = bf16[2,512,128,16]{1,3,2,0:T(8,128)(2,1)} copy(bf16[2,512,128,16]{2,1,0,3:T(8,128)(2,1)} %fusion.4) | data formatting | bytes 8388608 | tf_op jit(solution)/shard_map/convert_element_type | solution.py:135
  180.2 33.6 %reshape.292 = bf16[2,32,16,8,32,8]{2,1,5,4,3,0:T(8,128)(2,1)} reshape(bf16[2,512,128,16]{1,3,2,0:T(8,128)(2,1)} %copy.42) | data formatting | bytes 8388608 | tf_op jit(solution)/shard_map/reshape | solution.py:139
  213.8 30.6 %copy.43 = bf16[8,32,2,32,8,16]{3,5,4,2,1,0:T(8,128)(2,1)} copy(bf16[8,32,2,32,8,16]{5,3,4,1,0,2:T(8,128)(2,1)} %bitcast.71) | data formatting | bytes 8388608 | tf_op jit(solution)/shard_map/transpose | solution.py:140
  244.4 14.9 %copy.44 = bf16[8,32,2,32,128]{4,3,2,1,0:T(8,128)(2,1)} copy(bf16[8,32,2,32,128]{3,4,2,1,0:T(8,128)(2,1)} %bitcast.72) | data formatting | bytes 8388608 | tf_op jit(solution)/shard_map/reshape | solution.py:140
  259.4 0.0 copy-start.4
  259.4 0.0 copy-start.1
  259.4 0.0 copy-start.2
  259.4 0.0 copy-start.3
  259.4 98.4 %all_to_all.10 = bf16[8,32,2,32,128]{4,3,2,1,0:T(8,128)(2,1)} all-to-all(bf16[8,32,2,32,128]{4,3,2,1,0:T(8,128)(2,1)} %copy.44), channel_id=1, replica_groups=mesh['grp'=2,'chan'=2,'tm'=4,'pol'=2] {'chan','tm'}, dimensions={0} | all-to-all | bytes 8388608 | tf_op jit(solution)/shard_map/all_to_all | solution.py:143
  357.7 0.0 all-gather.3.cloned.1.call-update
  357.8 0.0 copy-done.4
  357.8 0.2 reduce-window.8
  358.0 0.0 copy-done.1
  358.0 0.0 copy-done.2
  358.0 0.1 pad_add_fusion
  358.1 0.1 fusion.30
  358.1 0.1 multiply_reduce_fusion.1
  358.2 0.2 copy.45.refs_0_
  358.5 0.0 copy-done.3
  358.5 0.1 multiply_reduce_fusion
  358.6 0.1 tile.9.refs_1_
  358.7 16.5 %all-gather.3.cloned.1.call-done = bf16[16,32,2,32,128]{4,3,2,1,0:T(8,128)(2,1)} async-done(((bf16[8,32,2,32,128]{4,3,2,1,0:T(8,128)(2,1)}), bf16[16,32,2,32,128]{4,3,2,1,0:T(8,128)(2,1)}) %all-gather.3.cloned.1.call-update) | async-done | bytes 8388624 | tf_op jit(solution)/shard_map/all_gather | solution.py:144
  375.2 52.6 %shard_map.64 = f32[8,32,2,2,64,128]{5,4,3,2,1,0:T(8,128)} custom-call(s32[8,128,1]{2,1,0:T(8,128)S(1)} %copy.45.refs_0_, f32[8,1,128]{2,1,0:T(1,128)S(1)} %tile.9.refs_1_, bf16[2,8,32,2,32,128]{5,4,3,2,1,0:T(8,128)(2,1)} %bitcast.75), custom_call_target="tpu_custom_call" | custom-call | tf_op jit(solution)/shard_map/pallas_call | solution.py:97
  (6 shorter events, 0.0 us)
Async XLA Ops:
  6.5 11.8 %copy-start = (f32[16,2048]{1,0:T(8,128)S(1)}, f32[16,2048]{1,0:T(8,128)}, u32[]{:S(2)}) copy-start(f32[16,2048]{1,0:T(8,128)} %param.7) | copy-start | bytes 393220
  11.2 99.7 %all-to-all-start = ((bf16[2,4,32,8192]{3,2,0,1:T(8,128)(2,1)}), bf16[2,4,32,8192]{3,2,0,1:T(8,128)(2,1)}, u32[]{:S(2)}, u32[]{:S(2)}) async-start(bf16[2,4,32,8192]{3,2,0,1:T(8,128)(2,1)} %copy.36), calls=%async_computation | async-start | bytes 8388608 | tf_op jit(solution)/shard_map/all_to_all | solution.py:125
  17.5 357.6 %all-gather.3.cloned.1.call-start = ((), (), s32[]{:S(2)}) async-start(), calls=%async_computation.2 | async-start | bytes 12582912 | tf_op jit(solution)/shard_map/all_gather | solution.py:144
  259.4 98.4 %copy-start.4 = (s32[14]{0:T(128)S(1)}, s32[14]{0:T(128)}, u32[]{:S(2)}) copy-start(s32[14]{0:T(128)} %param.10) | copy-start | bytes 172
  259.4 98.6 %copy-start.1 = (s32[14,64]{1,0:T(8,128)S(1)}, s32[14,64]{1,0:T(8,128)}, u32[]{:S(2)}) copy-start(s32[14,64]{1,0:T(8,128)} %param.9) | copy-start | bytes 10756
  259.4 98.6 %copy-start.2 = (s32[14,64]{1,0:T(8,128)S(1)}, s32[14,64]{1,0:T(8,128)}, u32[]{:S(2)}) copy-start(s32[14,64]{1,0:T(8,128)} %param.8) | copy-start | bytes 10756
  259.4 99.1 %copy-start.3 = (s32[14,16]{1,0:T(8,128)S(1)}, s32[14,16]{1,0:T(8,128)}, u32[]{:S(2)}) copy-start(s32[14,16]{1,0:T(8,128)} %param.11) | copy-start | bytes 2692
Sparse Core Ops, SparseCore 0:
  357.9 17.2 all-gather.2
where the time goes:
time: 438 us; the launch traced here: 435 us
  local copies, waits for them, and re-layouts  125 us (29%)
  waiting for transfers between devices  109 us (25%)
  blocking collectives  98.4 us (22%)
  Pallas kernels  52.6 us (12%)
  other arithmetic  15.6 us (4%)
  matrix products  14.6 us (3%)
  between operations  13.6 us (3%)
  starting transfers between devices  6.32 us (1%)
    all_to_all x1, blocking collectives, on_device(): lax.all_to_all(outgoing, ('chan', 'tm'), split_axis=0, concat_axis=0, til...  98.4 us
    all_to_all x1, waiting for transfers between devices, on_device(): lax.all_to_all(blocks, 'tm', split_axis=1, concat_axis=1, tiled=True)  92.5 us
    pallas_call x1, Pallas kernels, correlate(): pl.pallas_call(lambda *refs: correlate_kernel(step, sources * part_statio...  52.6 us
    reshape x1, local copies, waits for them, and re-layouts, on_device(): outgoing = spectra.reshape(2, share, spectra_count, owners, bands, AVG)  33.6 us
    transpose x1, local copies, waits for them, and re-layouts, on_device(): outgoing.transpose(3, 4, 0, 1, 5, 2)  30.6 us
    another operation x2, local copies, waits for them, and re-layouts, fourier(): grid = filtered.reshape(filtered.shape[:-1] + (radix_first, second))  20 us
    all_gather x1, waiting for transfers between devices, on_device(): full = lax.all_gather(moved, 'pol', axis=0)  16.5 us
    reshape x1, local copies, waits for them, and re-layouts, on_device(): outgoing.transpose(3, 4, 0, 1, 5, 2)  14.9 us
  transfers between devices with their start and end apart: 2, of which 2 were waited for; matrix products, arithmetic and copies ran while one was open for 0% of the time, Pallas kernels for 0%

commit v1 on v0

--- a/solution.py
+++ b/solution.py
@@ -1,6 +1,8 @@
 import math
 
 import jax
+import ml_dtypes
+import numpy as np
 import jax.numpy as jnp
 from jax import lax
 from jax.experimental import pallas as pl
@@ -44,6 +46,174 @@
         ]
     )
     return jnp.einsum("qrgj,rnfj->qngf", two, turned, precision=mode)
+
+
+def times(value, angle):
+    re, im = value
+    if angle % 16 == 0:
+        return re, im
+    c, s = math.cos(2.0 * math.pi * angle / 16), math.sin(2.0 * math.pi * angle / 16)
+    if angle % 16 == 4:
+        return im, -re
+    return re * c + im * s, im * c - re * s
+
+
+def four(x):
+    plus = [x[0][i] + x[2][i] for i in range(2)]
+    minus = [x[0][i] - x[2][i] for i in range(2)]
+    plus_odd = [x[1][i] + x[3][i] for i in range(2)]
+    minus_odd = [x[1][i] - x[3][i] for i in range(2)]
+    return [
+        (plus[0] + plus_odd[0], plus[1] + plus_odd[1]),
+        (minus[0] + minus_odd[1], minus[1] - minus_odd[0]),
+        (plus[0] - plus_odd[0], plus[1] - plus_odd[1]),
+        (minus[0] - minus_odd[1], minus[1] + minus_odd[0]),
+    ]
+
+
+def sixteen(x):
+    inner = [four([x[4 * a + b] for a in range(4)]) for b in range(4)]
+    result = [None] * 16
+    for c in range(4):
+        ends = four([times(inner[b][c], b * c) for b in range(4)])
+        for d in range(4):
+            result[c + 4 * d] = ends[d]
+    return result
+
+
+def spectra_kernel(x_ref, taps_ref, cos_ref, sin_ref, high_ref, low_ref, out_ref, held, turned):
+    time_count, block = x_ref.shape[1:3]
+    taps, length = taps_ref.shape
+    frames = x_ref.shape[3] // length
+    spectra_count = time_count * frames
+    second = length // radix_first
+    depth = AVG * spectra_count
+
+    def filter_section(k1, carry):
+        at = pl.multiple_of(k1 * second, second)
+        rows = [taps_ref[m : m + 1, pl.ds(at, second)] for m in range(taps)]
+        for r in range(2):
+            samples = []
+            for t in range(spectra_count):
+                place = pl.multiple_of(k1 * second + (t % frames) * length, second)
+                samples.append(x_ref[r, t // frames, :, pl.ds(place, second)].astype(jnp.float32))
+            filtered = []
+            for t in range(spectra_count):
+                total = rows[0] * samples[t]
+                for m in range(1, min(taps, t + 1)):
+                    total = total + rows[m] * samples[t - m]
+                filtered.append(total)
+            held[r, :, :, pl.ds(at, second)] = jnp.transpose(jnp.stack(filtered), (1, 0, 2))
+        return carry
+
+    lax.fori_loop(0, radix_first, filter_section, 0)
+
+    def transform_station(s, carry):
+        sections = [
+            tuple(held[r, s, :, k1 * second : (k1 + 1) * second] for r in range(2))
+            for k1 in range(radix_first)
+        ]
+        rows = []
+        for f1, (re, im) in enumerate(sixteen(sections)):
+            c, n = cos_ref[f1 : f1 + 1, :], sin_ref[f1 : f1 + 1, :]
+            rows.append(jnp.concatenate([re * c + im * n, im * c - re * n], axis=-1))
+        joined = jnp.concatenate(rows, axis=0)
+        high = joined.astype(jnp.bfloat16)
+        low = (joined - high.astype(jnp.float32)).astype(jnp.bfloat16)
+
+        def product(matrix, data):
+            return lax.dot_general(
+                matrix, data, (((1,), (1,)), ((), ())), preferred_element_type=jnp.float32
+            )
+
+        turned[s] = (
+            product(high_ref[...], high)
+            + product(high_ref[...], low)
+            + product(low_ref[...], high)
+        )
+        return carry
+
+    lax.fori_loop(0, block, transform_station, 0)
+
+    def place_channels(f, carry):
+        at = pl.multiple_of(f * 16, 16)
+        for q in range(2):
+            for h in range(radix_first // AVG):
+                part = turned[:, pl.ds(q * second + at, 16), h * depth : (h + 1) * depth]
+                out_ref[pl.ds(at, 16), h, q] = jnp.transpose(part, (1, 0, 2)).astype(jnp.bfloat16)
+        return carry
+
+    lax.fori_loop(0, second // 16, place_channels, 0)
+
+
+def local_spectra(blocks, taps_filter):
+    _, time_count, share, samples = blocks.shape
+    taps, length = taps_filter.shape
+    spectra_count = time_count * (samples // length)
+    second = length // radix_first
+    depth = AVG * spectra_count
+    block = 16
+    inner = np.arange(second)
+    twist = 2.0 * np.pi / length * (np.arange(radix_first)[:, None] * inner[None, :])
+    phase = 2.0 * np.pi / second * (inner[:, None] * inner[None, :] % second)
+    c, s = np.cos(phase) / math.sqrt(length), np.sin(phase) / math.sqrt(length)
+    matrix = np.block([[c, s], [-s, c]])
+    high = matrix.astype(ml_dtypes.bfloat16)
+    low = (matrix - high.astype(np.float64)).astype(ml_dtypes.bfloat16)
+    whole = lambda shape: pl.BlockSpec(shape, lambda i: (0, 0))
+    return pl.pallas_call(
+        spectra_kernel,
+        grid=(share // block,),
+        in_specs=[
+            pl.BlockSpec((2, time_count, block, samples), lambda i: (0, 0, i, 0)),
+            whole((taps, length)),
+            whole((radix_first, second)),
+            whole((radix_first, second)),
+            whole((2 * second, 2 * second)),
+            whole((2 * second, 2 * second)),
+        ],
+        out_specs=pl.BlockSpec(
+            (second, radix_first // AVG, 2, block, depth), lambda i: (0, 0, 0, i, 0)
+        ),
+        out_shape=jax.ShapeDtypeStruct(
+            (second, radix_first // AVG, 2, share, depth), jnp.bfloat16
+        ),
+        scratch_shapes=[
+            pltpu.VMEM((2, block, spectra_count, length), jnp.float32),
+            pltpu.VMEM((block, 2 * second, radix_first * spectra_count), jnp.float32),
+        ],
+        compiler_params=pltpu.CompilerParams(vmem_limit_bytes=48 * 2**20),
+    )(
+        blocks,
+        taps_filter,
+        np.cos(twist).astype(np.float32),
+        np.sin(twist).astype(np.float32),
+        high,
+        low,
+    )
+
+
+def plain_spectra(blocks, taps_filter):
+    _, time_count, share, samples = blocks.shape
+    taps, length = taps_filter.shape
+    frames = samples // length
+    spectra_count = time_count * frames
+    blocks = blocks.reshape(2, time_count, share, frames, length)
+    blocks = blocks.transpose(0, 2, 1, 3, 4).reshape(2, share, spectra_count, length)
+    extended = jnp.pad(blocks, ((0, 0), (0, 0), (taps - 1, 0), (0, 0)))
+    filtered = jnp.zeros((2, share, spectra_count, length), jnp.float32)
+    for tap_index in range(taps):
+        start = taps - 1 - tap_index
+        filtered = filtered + taps_filter[tap_index] * extended[
+            :, :, start : start + spectra_count
+        ].astype(jnp.float32)
+    spectra = fourier(filtered.reshape(2, share * spectra_count, length)).astype(jnp.bfloat16)
+    outgoing = spectra.reshape(
+        2, share, spectra_count, length // radix_first, radix_first // AVG, AVG
+    )
+    return outgoing.transpose(3, 4, 0, 1, 5, 2).reshape(
+        length // radix_first, radix_first // AVG, 2, share, AVG * spectra_count
+    )
 
 
 def correlate_kernel(bands, stations, rows_ref, weight_ref, full_ref, out_ref):
@@ -123,23 +293,11 @@
 
     blocks = voltages.reshape(2, time_count, share, frames * length)
     blocks = lax.all_to_all(blocks, "tm", split_axis=1, concat_axis=1, tiled=True)
-    blocks = blocks.reshape(2, time_count, share, frames, length)
-    blocks = blocks.transpose(0, 2, 1, 3, 4).reshape(2, share, spectra_count, length)
-    extended = jnp.pad(blocks, ((0, 0), (0, 0), (taps - 1, 0), (0, 0)))
-    filtered = jnp.zeros((2, share, spectra_count, length), jnp.float32)
-    for tap_index in range(taps):
-        start = taps - 1 - tap_index
-        filtered = filtered + taps_filter[tap_index] * extended[
-            :, :, start : start + spectra_count
-        ].astype(jnp.float32)
-    spectra = fourier(filtered.reshape(2, share * spectra_count, length)).astype(jnp.bfloat16)
+    spectra = (local_spectra if share % 16 == 0 else plain_spectra)(blocks, taps_filter)
 
     owners = chan_count * time_count
     bands = length // (owners * AVG)
-    outgoing = spectra.reshape(2, share, spectra_count, owners, bands, AVG)
-    outgoing = outgoing.transpose(3, 4, 0, 1, 5, 2).reshape(
-        owners, bands, 2, share, AVG * spectra_count
-    )
+    outgoing = spectra.reshape(owners, bands, 2, share, AVG * spectra_count)
     moved = lax.all_to_all(outgoing, ("chan", "tm"), split_axis=0, concat_axis=0, tiled=True)
     full = lax.all_gather(moved, "pol", axis=0)
 

time: 438 us -> 307 us (0.70)
  local copies, waits for them, and re-layouts: 125 us -> 5.73 us
  blocking collectives: 98.4 us -> 197 us
  waiting for transfers between devices: 109 us -> 15.9 us
  Pallas kernels: 52.6 us -> 74.4 us
  other arithmetic: 15.6 us -> 0.53 us
  matrix products: 14.6 us -> 0 us
  starting transfers between devices: 6.32 us -> 0.01 us
    all_to_all x0 -> x1, blocking collectives: none -> 99.3 us  [on_device(): lax.all_to_all(blocks, 'tm', split_axis=1, concat_axis=1, tiled=True)]
    all_to_all x1 -> x0, waiting for transfers between devices: 92.5 us -> none  [on_device(): lax.all_to_all(blocks, 'tm', split_axis=1, concat_axis=1, tiled=True)]
    reshape x3 -> x0, local copies, waits for them, and re-layouts: 56.3 us -> none  [the longest x1 33.6 us: on_device(): outgoing = spectra.reshape(2, share, spectra_count, owners, bands, AVG)]
    transpose x2 -> x0, local copies, waits for them, and re-layouts: 35.2 us -> none  [the longest x1 30.6 us: on_device(): outgoing.transpose(3, 4, 0, 1, 5, 2)]
    pallas_call x0 -> x1, Pallas kernels: none -> 21.8 us  [local_spectra(): pl.pallas_call(spectra_kernel, grid=(share // block,), in_specs=[pl.Block...]
    another operation x2 -> x0, local copies, waits for them, and re-layouts: 20 us -> none  [fourier(): grid = filtered.reshape(filtered.shape[:-1] + (radix_first, second))]
    dot_general x2 -> x0, matrix products: 14.6 us -> none  [the longest x1 8.49 us: fourier(): return jnp.einsum('qrgj,rnfj->qngf', two, turned, precision=mode)]
    add x2 -> x0, other arithmetic: 13.6 us -> none  [the longest x1 12.8 us: on_device(): filtered + taps_filter[tap_index] * extended[:, :, start:start + spectra_...]
  transfers between devices with their start and end apart: 2 -> 1, of which waited for: 2 -> 1; matrix products, arithmetic and copies ran while one was open for 0% -> 0% of each run, Pallas kernels for 0% -> 0%
where the time goes in v1:
time: 307 us
  blocking collectives  197 us (64%)
  Pallas kernels  74.4 us (24%)
  waiting for transfers between devices  15.9 us (5%)
  between operations  13.5 us (4%)
  local copies, waits for them, and re-layouts  5.73 us (2%)
    all_to_all x1, blocking collectives, on_device(): lax.all_to_all(blocks, 'tm', split_axis=1, concat_axis=1, tiled=True)  99.3 us
    all_to_all x1, blocking collectives, on_device(): lax.all_to_all(outgoing, ('chan', 'tm'), split_axis=0, concat_axis=0, til...  97.6 us
    pallas_call x1, Pallas kernels, correlate(): pl.pallas_call(lambda *refs: correlate_kernel(step, sources * part_statio...  52.6 us
    pallas_call x1, Pallas kernels, local_spectra(): pl.pallas_call(spectra_kernel, grid=(share // block,), in_specs=[pl.Block...  21.8 us
    all_gather x1, waiting for transfers between devices, on_device(): full = lax.all_gather(moved, 'pol', axis=0)  15.8 us
  transfers between devices with their start and end apart: 1, of which 1 were waited for; matrix products, arithmetic and copies ran while one was open for 0% of the time, Pallas kernels for 0%

profile of v1, /device:TPU:0, one launch (start us, length us, event | category | flops | bytes accessed | tf_op | source)
XLA Modules:
  0.0 306.8 jit_solution(15698930031740328254)
XLA Ops:
  6.5 0.0 all-gather.3.cloned.1.call-start
  6.5 2.5 copy.17
  9.0 99.3 %all_to_all.10 = bf16[2,4,32,8192]{3,2,0,1:T(8,128)(2,1)S(1)} all-to-all(bf16[2,4,32,8192]{3,2,0,1:T(8,128)(2,1)S(1)} %copy.17), channel_id=1, replica_groups=mesh['grp'=2,'chan'=2,'tm'=4,'pol'=2] {'tm'}, dimensions={1} | all-to-all | bytes 8388608 | tf_op jit(solution)/shard_map/all_to_all | solution.py:295
  108.3 0.0 copy-start
  108.3 0.0 copy-start.1
  108.3 0.0 copy-start.2
  108.3 0.0 copy-start.3
  108.3 0.0 copy-start.4
  108.3 2.3 copy.18.x_ref
  110.6 0.0 copy-done
  110.6 0.0 copy-done.1
  110.6 0.0 copy-done.2
  110.6 0.0 copy-done.3
  110.6 0.0 copy-done.4
  110.6 21.8 %shard_map.100 = bf16[128,2,2,32,128]{4,3,2,1,0:T(8,128)(2,1)S(1)} custom-call(bf16[2,4,32,8192]{3,2,1,0:T(8,128)(2,1)} %copy.18.x_ref, f32[16,2048]{1,0:T(8,128)S(1)} %copy-done, f32[16,128]{1,0:T(8,128)S(1)} %copy-done.4, f32[16,128]{1,0:T(8,128)S(1)} %copy-done.3, bf16[256,256]{1,0:T(8,128)(2,1)S(1)} %copy-done.2, bf16[256,256]{1,0:T(8,128)(2,1)S(1)} %copy-done.1), custom_call_target="tpu_custom_call" | custom-call | tf_op jit(solution)/shard_map/pallas_call | solution.py:164
  132.4 97.6 %all_to_all.11 = bf16[8,32,2,32,128]{4,3,2,1,0:T(8,128)(2,1)} all-to-all(bf16[8,32,2,32,128]{4,3,2,1,0:T(8,128)(2,1)S(1)} %bitcast.8), channel_id=1, replica_groups=mesh['grp'=2,'chan'=2,'tm'=4,'pol'=2] {'chan','tm'}, dimensions={0} | all-to-all | bytes 8388608 | tf_op jit(solution)/shard_map/all_to_all | solution.py:301
  230.0 0.0 copy-start.8
  230.0 0.0 copy-start.7
  230.0 0.0 copy-start.5
  230.0 0.0 copy-start.6
  230.0 0.0 all-gather.3.cloned.1.call-update
  230.1 0.6 copy-done.8
  230.7 0.2 reduce-window.8
  230.9 0.1 fusion.1
  231.0 0.0 copy-done.7
  231.0 0.1 multiply_reduce_fusion
  231.1 0.1 tile.9.refs_1_
  231.2 0.0 copy-done.5
  231.2 0.0 copy-done.6
  231.2 0.1 pad_add_fusion
  231.2 0.1 multiply_reduce_fusion.1
  231.3 0.2 copy.19.refs_0_
  231.6 15.8 %all-gather.3.cloned.1.call-done = bf16[16,32,2,32,128]{4,3,2,1,0:T(8,128)(2,1)} async-done(((bf16[8,32,2,32,128]{4,3,2,1,0:T(8,128)(2,1)}), bf16[16,32,2,32,128]{4,3,2,1,0:T(8,128)(2,1)}) %all-gather.3.cloned.1.call-update) | async-done | bytes 8388624 | tf_op jit(solution)/shard_map/all_gather | solution.py:302
  247.4 52.6 %shard_map.101 = f32[8,32,2,2,64,128]{5,4,3,2,1,0:T(8,128)} custom-call(s32[8,128,1]{2,1,0:T(8,128)S(1)} %copy.19.refs_0_, f32[8,1,128]{2,1,0:T(1,128)S(1)} %tile.9.refs_1_, bf16[2,8,32,2,32,128]{5,4,3,2,1,0:T(8,128)(2,1)} %bitcast.9), custom_call_target="tpu_custom_call" | custom-call | tf_op jit(solution)/shard_map/pallas_call | solution.py:267
  (4 shorter events, 0.0 us)
Async XLA Ops:
  6.5 240.9 %all-gather.3.cloned.1.call-start = ((), (), s32[]{:S(2)}) async-start(), calls=%async_computation.2 | async-start | bytes 12582912 | tf_op jit(solution)/shard_map/all_gather | solution.py:302
  108.3 2.3 copy-start
  108.3 2.3 copy-start.1
  108.3 2.3 copy-start.2
  108.3 2.3 copy-start.3
  108.3 2.3 copy-start.4
  230.0 0.7 copy-start.8
  230.0 0.9 copy-start.7
  230.0 1.1 copy-start.5
  230.0 1.1 copy-start.6
Sparse Core Ops, SparseCore 0:
  230.2 17.1 all-gather.2

commit v2 on v1

--- a/solution.py
+++ b/solution.py
@@ -216,12 +216,17 @@
     )
 
 
-def correlate_kernel(bands, stations, rows_ref, weight_ref, full_ref, out_ref):
-    width = rows_ref.shape[1] // 2
-    depth = full_ref.shape[-1]
-    columns = lax.broadcasted_iota(jnp.int32, (2 * width, stations), 1)
-    pick = jnp.where(rows_ref[0] == columns, 1.0, 0.0).astype(jnp.bfloat16)
-    weight = weight_ref[0]
+def correlate_kernel(rows_ref, weight_ref, full_ref, out_ref, pick):
+    pols, sources, bands, parts, part_stations, depth = full_ref.shape
+    stations = sources * part_stations
+    capacity = out_ref.shape[0]
+    width = out_ref.shape[4]
+
+    @pl.when(pl.program_id(0) == 0)
+    def _():
+        columns = lax.broadcasted_iota(jnp.int32, pick.shape, 1)
+        pick[...] = jnp.where(rows_ref[...] == columns, 1.0, 0.0).astype(jnp.bfloat16)
+
     for band in range(bands):
         source = jnp.concatenate(
             [
@@ -231,55 +236,56 @@
             ],
             axis=-1,
         )
-        picked = jnp.dot(pick, source, preferred_element_type=jnp.float32)
-        parts = [picked[:, i * depth : (i + 1) * depth] for i in range(4)]
-        left = [part[:width] * weight for part in parts]
-        right = [part[width:] for part in parts]
-        left_rows = jnp.concatenate(
-            [
-                jnp.concatenate([left[0], left[1]], axis=-1),
-                jnp.concatenate([left[2], left[3]], axis=-1),
-                jnp.concatenate([left[1], -left[0]], axis=-1),
-                jnp.concatenate([left[3], -left[2]], axis=-1),
-            ],
-            axis=0,
-        ).astype(jnp.bfloat16)
-        right_rows = jnp.concatenate(
-            [
-                jnp.concatenate([right[0], right[1]], axis=-1),
-                jnp.concatenate([right[2], right[3]], axis=-1),
-            ],
-            axis=0,
-        ).astype(jnp.bfloat16)
-        result = lax.dot_general(
-            left_rows,
-            right_rows,
-            (((1,), (1,)), ((), ())),
-            preferred_element_type=jnp.float32,
-        ) * (1.0 / depth)
-        out_ref[0, band] = result.reshape(2, 2, width, 2 * width)
+        picked = jnp.dot(pick[...], source, preferred_element_type=jnp.float32).astype(
+            jnp.bfloat16
+        )
+        for slot in range(capacity):
+            at = 2 * width * slot
+            weight = weight_ref[slot]
+            left = [
+                picked[at : at + width, i * depth : (i + 1) * depth] * weight for i in range(4)
+            ]
+            other = picked[at + width : at + 2 * width]
+            left_rows = jnp.concatenate(
+                [
+                    jnp.concatenate([left[0], left[1]], axis=-1),
+                    jnp.concatenate([left[2], left[3]], axis=-1),
+                    jnp.concatenate([left[1], -left[0]], axis=-1),
+                    jnp.concatenate([left[3], -left[2]], axis=-1),
+                ],
+                axis=0,
+            )
+            right_rows = jnp.concatenate([other[:, : 2 * depth], other[:, 2 * depth :]], axis=0)
+            result = lax.dot_general(
+                left_rows,
+                right_rows,
+                (((1,), (1,)), ((), ())),
+                preferred_element_type=jnp.float32,
+            ) * (1.0 / depth)
+            out_ref[slot, band] = result.reshape(2, 2, width, 2 * width)
 
 
 def correlate(full, rows, weight):
     pols, sources, bands, parts, part_stations, depth = full.shape
     width = rows.shape[1] // 2
-    step = 4 if bands % 4 == 0 else 1
+    step = 2 if bands % 2 == 0 and bands > 2 else 1
     return pl.pallas_call(
-        lambda *refs: correlate_kernel(step, sources * part_stations, *refs),
-        grid=(bands // step, CAP),
+        correlate_kernel,
+        grid=(bands // step,),
         in_specs=[
-            pl.BlockSpec((1, 2 * width, 1), lambda g, n: (n, 0, 0)),
-            pl.BlockSpec((1, 1, depth), lambda g, n: (n, 0, 0)),
+            pl.BlockSpec((CAP * 2 * width, 1), lambda g: (0, 0)),
+            pl.BlockSpec((CAP, 1, depth), lambda g: (0, 0, 0)),
             pl.BlockSpec(
-                (pols, sources, step, parts, part_stations, depth), lambda g, n: (0, 0, g, 0, 0, 0)
+                (pols, sources, step, parts, part_stations, depth), lambda g: (0, 0, g, 0, 0, 0)
             ),
         ],
         out_specs=pl.BlockSpec(
-            (1, step, 2, 2, width, 2 * width), lambda g, n: (n, g, 0, 0, 0, 0)
+            (CAP, step, 2, 2, width, 2 * width), lambda g: (0, g, 0, 0, 0, 0)
         ),
         out_shape=jax.ShapeDtypeStruct((CAP, bands, 2, 2, width, 2 * width), jnp.float32),
+        scratch_shapes=[pltpu.VMEM((CAP * 2 * width, sources * part_stations), jnp.bfloat16)],
         compiler_params=pltpu.CompilerParams(vmem_limit_bytes=48 * 2**20),
-    )(rows, weight, full)
+    )(rows.reshape(CAP * 2 * width, 1), weight.astype(jnp.bfloat16), full)
 
 
 def on_device(voltages, taps_filter, tile_a, tile_b, tile_owner, tile_flags):

time: 307 us -> 279 us (0.909)
  Pallas kernels: 74.4 us -> 46.1 us
    pallas_call x1, Pallas kernels: 52.6 us -> 24.3 us  [correlate(): pl.pallas_call(correlate_kernel, grid=(bands // step,), in_specs=[pl.Bloc...]
where the time goes in v2:
time: 279 us
  blocking collectives  197 us (71%)
  Pallas kernels  46.1 us (17%)
  waiting for transfers between devices  15.9 us (6%)
  between operations  13.5 us (5%)
  local copies, waits for them, and re-layouts  5.73 us (2%)
    all_to_all x1, blocking collectives, on_device(): lax.all_to_all(blocks, 'tm', split_axis=1, concat_axis=1, tiled=True)  99.3 us
    all_to_all x1, blocking collectives, on_device(): lax.all_to_all(outgoing, ('chan', 'tm'), split_axis=0, concat_axis=0, til...  97.6 us
    pallas_call x1, Pallas kernels, correlate(): pl.pallas_call(correlate_kernel, grid=(bands // step,), in_specs=[pl.Bloc...  24.3 us
    pallas_call x1, Pallas kernels, local_spectra(): pl.pallas_call(spectra_kernel, grid=(share // block,), in_specs=[pl.Block...  21.8 us
    all_gather x1, waiting for transfers between devices, on_device(): full = lax.all_gather(moved, 'pol', axis=0)  15.8 us
  transfers between devices with their start and end apart: 1, of which 1 were waited for; matrix products, arithmetic and copies ran while one was open for 0% of the time, Pallas kernels for 0%

profile of v2, /device:TPU:0, one launch (start us, length us, event | category | flops | bytes accessed | tf_op | source)
XLA Modules:
  0.0 278.6 jit_solution(3156677738810255064)
XLA Ops:
  6.5 0.0 all-gather.3.cloned.1.call-start
  6.5 2.5 copy.20
  9.0 99.3 %all_to_all.10 = bf16[2,4,32,8192]{3,2,0,1:T(8,128)(2,1)S(1)} all-to-all(bf16[2,4,32,8192]{3,2,0,1:T(8,128)(2,1)S(1)} %copy.20), channel_id=1, replica_groups=mesh['grp'=2,'chan'=2,'tm'=4,'pol'=2] {'tm'}, dimensions={1} | all-to-all | bytes 8388608 | tf_op jit(solution)/shard_map/all_to_all | solution.py:301
  108.3 0.0 copy-start
  108.3 0.0 copy-start.1
  108.3 0.0 copy-start.2
  108.3 0.0 copy-start.3
  108.3 0.0 copy-start.4
  108.3 2.3 copy.21.x_ref
  110.6 0.0 copy-done
  110.6 0.0 copy-done.1
  110.6 0.0 copy-done.2
  110.6 0.0 copy-done.3
  110.6 0.0 copy-done.4
  110.6 21.8 %shard_map.100 = bf16[128,2,2,32,128]{4,3,2,1,0:T(8,128)(2,1)S(1)} custom-call(bf16[2,4,32,8192]{3,2,1,0:T(8,128)(2,1)} %copy.21.x_ref, f32[16,2048]{1,0:T(8,128)S(1)} %copy-done, f32[16,128]{1,0:T(8,128)S(1)} %copy-done.4, f32[16,128]{1,0:T(8,128)S(1)} %copy-done.3, bf16[256,256]{1,0:T(8,128)(2,1)S(1)} %copy-done.2, bf16[256,256]{1,0:T(8,128)(2,1)S(1)} %copy-done.1), custom_call_target="tpu_custom_call" | custom-call | tf_op jit(solution)/shard_map/pallas_call | solution.py:164
  132.4 97.6 %all_to_all.11 = bf16[8,32,2,32,128]{4,3,2,1,0:T(8,128)(2,1)} all-to-all(bf16[8,32,2,32,128]{4,3,2,1,0:T(8,128)(2,1)S(1)} %bitcast.8), channel_id=1, replica_groups=mesh['grp'=2,'chan'=2,'tm'=4,'pol'=2] {'chan','tm'}, dimensions={0} | all-to-all | bytes 8388608 | tf_op jit(solution)/shard_map/all_to_all | solution.py:307
  230.0 0.0 copy-start.8
  230.0 0.0 copy-start.7
  230.0 0.0 copy-start.5
  230.0 0.0 copy-start.6
  230.0 0.0 all-gather.3.cloned.1.call-update
  230.1 0.6 copy-done.8
  230.7 0.2 reduce-window.8
  230.9 0.1 fusion.1
  231.0 0.0 copy-done.7
  231.0 0.1 multiply_reduce_fusion
  231.1 0.1 convert_element_type.24.weight_ref
  231.2 0.0 copy-done.5
  231.2 0.0 copy-done.6
  231.2 0.1 pad_add_fusion
  231.3 0.1 multiply_reduce_fusion.1
  231.3 0.2 copy.22.rows_ref
  231.6 15.8 %all-gather.3.cloned.1.call-done = bf16[16,32,2,32,128]{4,3,2,1,0:T(8,128)(2,1)} async-done(((bf16[8,32,2,32,128]{4,3,2,1,0:T(8,128)(2,1)}), bf16[16,32,2,32,128]{4,3,2,1,0:T(8,128)(2,1)}) %all-gather.3.cloned.1.call-update) | async-done | bytes 8388624 | tf_op jit(solution)/shard_map/all_gather | solution.py:308
  247.4 24.3 %shard_map.101 = f32[8,32,2,2,64,128]{5,4,3,2,1,0:T(8,128)} custom-call(s32[1024,1]{1,0:T(8,128)S(1)} %copy.22.rows_ref, bf16[8,1,128]{2,1,0:T(2,128)(2,1)S(1)} %convert_element_type.24.weight_ref, bf16[2,8,32,2,32,128]{5,4,3,2,1,0:T(8,128)(2,1)} %bitcast.9), custom_call_target="tpu_custom_call" | custom-call | tf_op jit(solution)/shard_map/pallas_call | solution.py:272
  (4 shorter events, 0.0 us)
Async XLA Ops:
  6.5 240.9 %all-gather.3.cloned.1.call-start = ((), (), s32[]{:S(2)}) async-start(), calls=%async_computation.2 | async-start | bytes 12582912 | tf_op jit(solution)/shard_map/all_gather | solution.py:308
  108.3 2.3 copy-start
  108.3 2.3 copy-start.1
  108.3 2.3 copy-start.2
  108.3 2.3 copy-start.3
  108.3 2.3 copy-start.4
  230.0 0.7 copy-start.8
  230.0 0.9 copy-start.7
  230.0 1.1 copy-start.5
  230.0 1.1 copy-start.6
Sparse Core Ops, SparseCore 0:
  230.2 17.1 all-gather.2

commit v3 on v2

--- a/solution.py
+++ b/solution.py
@@ -216,8 +216,8 @@
     )
 
 
-def correlate_kernel(rows_ref, weight_ref, full_ref, out_ref, pick):
-    pols, sources, bands, parts, part_stations, depth = full_ref.shape
+def correlate_kernel(place_ref, rows_ref, weight_ref, own_ref, other_ref, out_ref, pick, source):
+    sources, bands, parts, part_stations, depth = own_ref.shape
     stations = sources * part_stations
     capacity = out_ref.shape[0]
     width = out_ref.shape[4]
@@ -228,15 +228,12 @@
         pick[...] = jnp.where(rows_ref[...] == columns, 1.0, 0.0).astype(jnp.bfloat16)
 
     for band in range(bands):
-        source = jnp.concatenate(
-            [
-                full_ref[p, :, band, r].reshape(stations, depth)
-                for p in range(2)
-                for r in range(2)
-            ],
-            axis=-1,
-        )
-        picked = jnp.dot(pick[...], source, preferred_element_type=jnp.float32).astype(
+        for ref, polarisation in ((own_ref, place_ref[0]), (other_ref, 1 - place_ref[0])):
+            at = pl.multiple_of(polarisation * (2 * depth), depth)
+            source[band, :, pl.ds(at, 2 * depth)] = jnp.concatenate(
+                [ref[:, band, r].reshape(stations, depth) for r in range(2)], axis=-1
+            )
+        picked = jnp.dot(pick[...], source[band], preferred_element_type=jnp.float32).astype(
             jnp.bfloat16
         )
         for slot in range(capacity):
@@ -265,27 +262,30 @@
             out_ref[slot, band] = result.reshape(2, 2, width, 2 * width)
 
 
-def correlate(full, rows, weight):
-    pols, sources, bands, parts, part_stations, depth = full.shape
+def correlate(place, own, other, rows, weight):
+    sources, bands, parts, part_stations, depth = own.shape
     width = rows.shape[1] // 2
     step = 2 if bands % 2 == 0 and bands > 2 else 1
     return pl.pallas_call(
         correlate_kernel,
         grid=(bands // step,),
         in_specs=[
+            pl.BlockSpec(memory_space=pltpu.SMEM),
             pl.BlockSpec((CAP * 2 * width, 1), lambda g: (0, 0)),
             pl.BlockSpec((CAP, 1, depth), lambda g: (0, 0, 0)),
-            pl.BlockSpec(
-                (pols, sources, step, parts, part_stations, depth), lambda g: (0, 0, g, 0, 0, 0)
-            ),
+            pl.BlockSpec((sources, step, parts, part_stations, depth), lambda g: (0, g, 0, 0, 0)),
+            pl.BlockSpec((sources, step, parts, part_stations, depth), lambda g: (0, g, 0, 0, 0)),
         ],
         out_specs=pl.BlockSpec(
             (CAP, step, 2, 2, width, 2 * width), lambda g: (0, g, 0, 0, 0, 0)
         ),
         out_shape=jax.ShapeDtypeStruct((CAP, bands, 2, 2, width, 2 * width), jnp.float32),
-        scratch_shapes=[pltpu.VMEM((CAP * 2 * width, sources * part_stations), jnp.bfloat16)],
+        scratch_shapes=[
+            pltpu.VMEM((CAP * 2 * width, sources * part_stations), jnp.bfloat16),
+            pltpu.VMEM((step, sources * part_stations, 4 * depth), jnp.bfloat16),
+        ],
         compiler_params=pltpu.CompilerParams(vmem_limit_bytes=48 * 2**20),
-    )(rows.reshape(CAP * 2 * width, 1), weight.astype(jnp.bfloat16), full)
+    )(place, rows.reshape(CAP * 2 * width, 1), weight.astype(jnp.bfloat16), own, other)
 
 
 def on_device(voltages, taps_filter, tile_a, tile_b, tile_owner, tile_flags):
@@ -305,7 +305,7 @@
     bands = length // (owners * AVG)
     outgoing = spectra.reshape(owners, bands, 2, share, AVG * spectra_count)
     moved = lax.all_to_all(outgoing, ("chan", "tm"), split_axis=0, concat_axis=0, tiled=True)
-    full = lax.all_gather(moved, "pol", axis=0)
+    other = lax.ppermute(moved, "pol", [(0, 1), (1, 0)])
 
     position = lax.axis_index("pol")
     held = tile_owner == position
@@ -317,7 +317,7 @@
     rows = jnp.sum(chosen[:, :, None] * pairs[None], axis=1)[:, :, None]
     flags = jnp.sum(chosen[:, :, None] * tile_flags[None], axis=1)
     weight = jnp.tile(flags.astype(jnp.float32), (1, AVG))[:, None, :]
-    return correlate(full, rows, weight)
+    return correlate(position.reshape(1).astype(jnp.int32), moved, other, rows, weight)
 
 
 def solution(mesh):

time: 279 us -> 256 us (0.918)
  between operations: 13.5 us -> 0.12 us
  waiting for transfers between devices: 15.9 us -> 6.6 us
    all_gather x1 -> x0, waiting for transfers between devices: 15.8 us -> none  [on_device(): full = lax.all_gather(moved, 'pol', axis=0)]
    ppermute x0 -> x1, waiting for transfers between devices: none -> 6.6 us  [on_device(): other = lax.ppermute(moved, 'pol', [(0, 1), (1, 0)])]
where the time goes in v3:
time: 256 us; the launch traced here: 255 us
  blocking collectives  197 us (77%)
  Pallas kernels  46.1 us (18%)
  waiting for transfers between devices  6.6 us (3%)
  local copies, waits for them, and re-layouts  5.11 us (2%)
    all_to_all x1, blocking collectives, on_device(): lax.all_to_all(blocks, 'tm', split_axis=1, concat_axis=1, tiled=True)  99.3 us
    all_to_all x1, blocking collectives, on_device(): lax.all_to_all(outgoing, ('chan', 'tm'), split_axis=0, concat_axis=0, til...  97.8 us
    pallas_call x1, Pallas kernels, correlate(): pl.pallas_call(correlate_kernel, grid=(bands // step,), in_specs=[pl.Bloc...  24.4 us
    pallas_call x1, Pallas kernels, local_spectra(): pl.pallas_call(spectra_kernel, grid=(share // block,), in_specs=[pl.Block...  21.7 us
    ppermute x1, waiting for transfers between devices, on_device(): other = lax.ppermute(moved, 'pol', [(0, 1), (1, 0)])  6.6 us
  transfers between devices with their start and end apart: 1, of which 1 were waited for; matrix products, arithmetic and copies ran while one was open for 0% of the time, Pallas kernels for 0%

profile of v3, /device:TPU:0, one launch (start us, length us, event | category | flops | bytes accessed | tf_op | source)
XLA Modules:
  0.0 255.5 jit_solution(18003424966231885678)
XLA Ops:
  0.0 2.5 copy.20
  2.5 99.3 %all_to_all.10 = bf16[2,4,32,8192]{3,2,0,1:T(8,128)(2,1)S(1)} all-to-all(bf16[2,4,32,8192]{3,2,0,1:T(8,128)(2,1)S(1)} %copy.20), channel_id=1, replica_groups=mesh['grp'=2,'chan'=2,'tm'=4,'pol'=2] {'tm'}, dimensions={1} | all-to-all | bytes 8388608 | tf_op jit(solution)/shard_map/all_to_all | solution.py:301
  101.7 0.0 copy-start
  101.7 0.0 copy-start.1
  101.7 0.0 copy-start.2
  101.7 0.0 copy-start.3
  101.7 0.0 copy-start.4
  101.7 2.3 copy.21.x_ref
  104.0 0.0 copy-done
  104.0 0.0 copy-done.1
  104.0 0.0 copy-done.2
  104.0 0.0 copy-done.3
  104.0 0.0 copy-done.4
  104.1 21.7 %shard_map.100 = bf16[128,2,2,32,128]{4,3,2,1,0:T(8,128)(2,1)S(1)} custom-call(bf16[2,4,32,8192]{3,2,1,0:T(8,128)(2,1)} %copy.21.x_ref, f32[16,2048]{1,0:T(8,128)S(1)} %copy-done, f32[16,128]{1,0:T(8,128)S(1)} %copy-done.4, f32[16,128]{1,0:T(8,128)S(1)} %copy-done.3, bf16[256,256]{1,0:T(8,128)(2,1)S(1)} %copy-done.2, bf16[256,256]{1,0:T(8,128)(2,1)S(1)} %copy-done.1), custom_call_target="tpu_custom_call" | custom-call | tf_op jit(solution)/shard_map/pallas_call | solution.py:164
  125.7 0.0 copy-start.8
  125.8 0.0 copy-start.7
  125.8 0.0 copy-start.5
  125.8 0.0 copy-start.6
  125.8 97.8 %all_to_all.11.own_ref = bf16[8,32,2,32,128]{4,3,2,1,0:T(8,128)(2,1)} all-to-all(bf16[8,32,2,32,128]{4,3,2,1,0:T(8,128)(2,1)S(1)} %bitcast.8), channel_id=1, replica_groups=mesh['grp'=2,'chan'=2,'tm'=4,'pol'=2] {'chan','tm'}, dimensions={0} | all-to-all | bytes 8388608 | tf_op jit(solution)/shard_map/all_to_all | solution.py:307
  223.6 0.0 collective-permute-start
  223.6 0.0 copy-done.8
  223.6 0.2 reduce-window.8
  223.8 0.1 fusion.1
  223.9 0.0 copy-done.7
  223.9 0.1 multiply_reduce_fusion
  224.0 0.1 convert_element_type.24.weight_ref
  224.1 0.0 copy-done.5
  224.1 0.0 copy-done.6
  224.1 0.1 pad_add_fusion
  224.2 0.1 multiply_reduce_fusion.1
  224.2 0.2 copy.22.rows_ref
  224.5 6.6 %collective-permute-done.other_ref = bf16[8,32,2,32,128]{4,3,2,1,0:T(8,128)(2,1)} collective-permute-done((bf16[8,32,2,32,128]{4,3,2,1,0:T(8,128)(2,1)}, bf16[8,32,2,32,128]{4,3,2,1,0:T(8,128)(2,1)}, u32[]{:S(2)}, u32[]{:S(2)}) %collective-permute-start) | collective-permute-done | bytes 4194336 | tf_op jit(solution)/shard_map/ppermute | solution.py:308
  231.1 24.4 %shard_map.101 = f32[8,32,2,2,64,128]{5,4,3,2,1,0:T(8,128)} custom-call(s32[1]{0:T(128)} %bitcast.place_ref, s32[1024,1]{1,0:T(8,128)S(1)} %copy.22.rows_ref, bf16[8,1,128]{2,1,0:T(2,128)(2,1)S(1)} %convert_element_type.24.weight_ref, bf16[8,32,2,32,128]{4,3,2,1,0:T(8,128)(2,1)} %all_to_all.11.own_ref, ...), custom_call_target="tpu_custom_call" | custom-call | tf_op jit(solution)/shard_map/pallas_call | solution.py:269
  (4 shorter events, 0.0 us)
Async XLA Ops:
  101.7 2.3 copy-start
  101.7 2.3 copy-start.1
  101.7 2.3 copy-start.2
  101.7 2.3 copy-start.3
  101.7 2.3 copy-start.4
  125.7 97.8 %copy-start.8 = (s32[14]{0:T(128)S(1)}, s32[14]{0:T(128)}, u32[]{:S(2)}) copy-start(s32[14]{0:T(128)} %param.14) | copy-start | bytes 172
  125.8 98.1 %copy-start.7 = (s32[14,16]{1,0:T(8,128)S(1)}, s32[14,16]{1,0:T(8,128)}, u32[]{:S(2)}) copy-start(s32[14,16]{1,0:T(8,128)} %param.15) | copy-start | bytes 2692
  125.8 98.3 %copy-start.5 = (s32[14,64]{1,0:T(8,128)S(1)}, s32[14,64]{1,0:T(8,128)}, u32[]{:S(2)}) copy-start(s32[14,64]{1,0:T(8,128)} %param.13) | copy-start | bytes 10756
  125.8 98.3 %copy-start.6 = (s32[14,64]{1,0:T(8,128)S(1)}, s32[14,64]{1,0:T(8,128)}, u32[]{:S(2)}) copy-start(s32[14,64]{1,0:T(8,128)} %param.12) | copy-start | bytes 10756
  223.6 7.5 %collective-permute-start = (bf16[8,32,2,32,128]{4,3,2,1,0:T(8,128)(2,1)}, bf16[8,32,2,32,128]{4,3,2,1,0:T(8,128)(2,1)}, u32[]{:S(2)}, u32[]{:S(2)}) collective-permute-start(bf16[8,32,2,32,128]{4,3,2,1,0:T(8,128)(2,1)} %all_to_all.11.own_ref), channel_id=1, source_target_pairs={{0,1},{1,0},{2,3},{3,2},{4,5},{5,4},{6,7},{7,6},{8,9},{9,8},{10,11... | collective-permute-start | bytes 12582920 | tf_op jit(solution)/shard_map/ppermute | solution.py:308
